TPU v7x, 32 devices: a whole 2x2x4 slice. The times are simulated.
32 devices in a mesh: dp: 4 (over y, x), row: 2 (over core), col: 4 (over z).
Axes of the slice: x: 2, y: 2, z: 4, core: 2. Of those that a mesh axis runs over, the one named last changes fastest.
Arguments:
- tokens: bfloat16 [1280, 16384], P('row', ('dp', 'col')), may hold values from -6 to 6
- segment_ids: int32 [8, 2048], P(('dp', 'row')), may hold values from 0 to 3, never falling along the last dimension, each value on 1 to 1024 neighbouring positions
- padding_mask: int32 [8, 2048], P(('dp', 'row')), may hold values from 0 to 1, as said below
- w_qkv: bfloat16 [4915200], P(('row', 'col')), may hold values from -0.15625 to 0.15625
- w_out: bfloat16 [1638400], P(('row', 'col')), may hold values from -1.25 to 1.25
- w_up: bfloat16 [1638400], P(('row', 'col')), may hold values from -0.15625 to 0.15625
- w_down: bfloat16 [1638400], P(('row', 'col')), may hold values from -0.15625 to 0.15625
- gain_attn: float32 [1280], replicated, may hold values from 0.5 to 1.5
- gain_mlp: float32 [1280], replicated, may hold values from 0.5 to 1.5
- scale_raw: float32 [80], replicated, may hold values from -0.5 to 1.5
- cotangent: bfloat16 [1280, 16384], P('row', ('dp', 'col')), may hold values from -6 to 6
Outputs:
- result: float32 [1280, 16384], P('row', ('dp', 'col'))
- grad_tokens: float32 [1280, 16384], P('row', ('dp', 'col'))
- grad_qkv: float32 [4915200], P(('row', 'col'))
- grad_wout: float32 [1638400], P(('row', 'col'))
- grad_up: float32 [1638400], P(('row', 'col'))
- grad_down: float32 [1638400], P(('row', 'col'))
- grad_gain_attn: float32 [1280], replicated
- grad_gain_mlp: float32 [1280], replicated
- grad_scale: float32 [80], replicated
Inputs may be any that keep to these rules, and one draw needn't show every extreme that they name: `segment_ids`: within each row the document numbers never fall; a document holds at most 1024 tokens. `padding_mask`: each row is a nonempty run of ones followed by a nonempty run of zeros.
All inputs are finite; a program needn't handle non-finite values.
Results may differ from a plain program's by a relative error of at most 0.012.
The roundings to bfloat16 on the way count: a program that leaves them out, or rounds other values in their place, can miss the bound.
Values may be sent and summed in bfloat16 or wider, within the bound.
A program may use at most 256 MiB of HBM per device.

v0:
```python
import math

import jax
import jax.numpy as jnp
from jax import lax
from jax.sharding import PartitionSpec as P

D = 1280
HEAD = 80


EPSILON = 1e-06
LOG_TWO_E = 1.442695041
row_block = 512
contract_rows = (((0,), (0,)), ((), ()))
contract_last = (((1,), (1,)), ((), ()))


def row_total(values):
    return lax.psum(values, "row")


def across_col(piece):
    return lax.all_gather(piece, "col", axis=0, tiled=True)


def across_row(piece):
    return lax.all_gather(piece, "row", axis=0, tiled=True)


def sum_rows(product, number):
    return lax.psum_scatter(
        product(jnp.int32(0), number * lax.axis_size("row")), "row", scatter_dimension=0, tiled=True
    )


def sum_cols(product, number):
    return lax.psum_scatter(
        product(jnp.int32(0), number * lax.axis_size("col")), "col", scatter_dimension=0, tiled=True
    )


def norm_forward(inputs, gain_block):
    squares = row_total(jnp.sum(inputs * inputs, axis=1))
    inverse = lax.rsqrt(squares / D + EPSILON)[:, None]
    return (inverse, (inputs * inverse * gain_block).astype(jnp.bfloat16))


def norm_backward(inputs, inverse, gain_block, grad_normed):
    scaled = grad_normed * gain_block
    inner = row_total(jnp.sum(scaled * inputs, axis=1))[:, None]
    grad_inputs = inverse * scaled - inputs * inverse * inverse * inverse * inner / D
    grad_gain = jnp.sum(grad_normed * inputs * inverse, axis=0)
    return (grad_inputs, grad_gain)


def project_in(normed, weight_block):
    gathered = across_col(normed)
    length = gathered.shape[0] // lax.axis_size("row")

    def piece_term(offset, number):
        return jnp.dot(gathered, weight_block, preferred_element_type=jnp.float32)

    return (gathered, sum_rows(piece_term, length))


def project_out(activations, weight_block):
    gathered = across_row(activations)
    share_rows = gathered.shape[0] // lax.axis_size("col")

    def piece_term(offset, number):
        return jnp.dot(gathered, weight_block, preferred_element_type=jnp.float32)

    return (gathered, sum_cols(piece_term, share_rows))


def back_out(grad_branch, gathered_values, weight_block):
    gathered_grad = across_col(grad_branch)
    grad_weight = lax.dot_general(
        gathered_values, gathered_grad, contract_rows, preferred_element_type=jnp.float32
    )
    length = gathered_grad.shape[0] // lax.axis_size("row")

    def piece_term(offset, number):
        return lax.dot_general(
            gathered_grad, weight_block, contract_last, preferred_element_type=jnp.float32
        )

    return (sum_rows(piece_term, length), grad_weight)


def back_in(grad_hidden, gathered_inputs, weight_block):
    gathered_grad = across_row(grad_hidden)
    grad_weight = lax.dot_general(
        gathered_inputs, gathered_grad, contract_rows, preferred_element_type=jnp.float32
    )
    share_rows = gathered_grad.shape[0] // lax.axis_size("col")

    def piece_term(offset, number):
        return lax.dot_general(
            gathered_grad, weight_block, contract_last, preferred_element_type=jnp.float32
        )

    return (sum_cols(piece_term, share_rows), grad_weight)


def allowed_block(segments, padding, offset, number):
    positions = lax.iota(jnp.int32, segments.shape[0])
    row_places = offset + lax.iota(jnp.int32, number)
    seg_rows = lax.dynamic_slice_in_dim(segments, offset, number, 0)
    matching = seg_rows[:, None] == segments[None, :]
    causal = positions[None, :] <= row_places[:, None]
    visible = (padding[None, :] == 1) | (positions[None, :] == row_places[:, None])
    return matching & causal & visible


def block_scores(query_rows, key_heads, segments, padding, offset, number):
    scores = jnp.einsum("qhe,khe->hqk", query_rows, key_heads, preferred_element_type=jnp.float32)
    return jnp.where(allowed_block(segments, padding, offset, number)[None], scores, -1e30)


def attention_forward(queries, key_heads, values, segments, padding):
    length = queries.shape[0]
    block_size = min(row_block, length)

    def one_block(block_index):
        offset = block_index * block_size
        query_rows = lax.dynamic_slice_in_dim(queries, offset, block_size, 0)
        scores = block_scores(query_rows, key_heads, segments, padding, offset, block_size)
        row_peak = jnp.max(scores, axis=2, keepdims=True)
        exponent = jnp.exp(scores - row_peak)
        denominator = jnp.sum(exponent, axis=2, keepdims=True)
        weights_low = (exponent / denominator).astype(jnp.bfloat16)
        attended_rows = jnp.einsum(
            "hqk,khe->qhe", weights_low, values, preferred_element_type=jnp.float32
        )
        return (attended_rows, (row_peak + jnp.log(denominator))[:, :, 0])

    attended, log_totals = lax.map(one_block, jnp.arange(length // block_size, dtype=jnp.int32))
    return (attended.reshape(length, -1), log_totals)


def attention_backward(queries, key_heads, values, segments, padding, log_totals, grad_attended):
    length, heads_here, head_size = queries.shape
    block_size = min(row_block, length)

    def one_block(carried, pieces):
        grad_keys, grad_values = carried
        block_index, log_block = pieces
        offset = block_index * block_size
        query_rows = lax.dynamic_slice_in_dim(queries, offset, block_size, 0)
        grad_rows = lax.dynamic_slice_in_dim(grad_attended, offset, block_size, 0)
        scores = block_scores(query_rows, key_heads, segments, padding, offset, block_size)
        probability = jnp.exp(scores - log_block[:, :, None])
        grad_prob = jnp.einsum(
            "qhe,khe->hqk", grad_rows, values, preferred_element_type=jnp.float32
        )
        inner = jnp.sum(probability * grad_prob, axis=2, keepdims=True)
        grad_scores = (probability * (grad_prob - inner)).astype(jnp.bfloat16)
        grad_query_rows = jnp.einsum(
            "hqk,khe->qhe", grad_scores, key_heads, preferred_element_type=jnp.float32
        )
        grad_keys = grad_keys + jnp.einsum(
            "hqk,qhe->khe", grad_scores, query_rows, preferred_element_type=jnp.float32
        )
        grad_values = grad_values + jnp.einsum(
            "hqk,qhe->khe",
            probability.astype(jnp.bfloat16),
            grad_rows,
            preferred_element_type=jnp.float32,
        )
        return ((grad_keys, grad_values), grad_query_rows)

    empty = jnp.zeros((length, heads_here, head_size), jnp.float32)
    steps_index = jnp.arange(length // block_size, dtype=jnp.int32)
    (grad_keys, grad_values), grad_queries = lax.scan(
        one_block, (empty, empty), (steps_index, log_totals)
    )
    return (grad_queries.reshape(length, heads_here, head_size), grad_keys, grad_values)


def on_device(
    tokens,
    segment_ids,
    padding_mask,
    w_qkv,
    w_out,
    w_up,
    w_down,
    gain_attn,
    gain_mlp,
    scale_raw,
    cotangent,
):
    width_share = tokens.shape[0]
    feature_start = lax.axis_index("row") * width_share
    gain_one = lax.dynamic_slice_in_dim(gain_attn, feature_start, width_share, 0)
    gain_two = lax.dynamic_slice_in_dim(gain_mlp, feature_start, width_share, 0)
    inputs = tokens.astype(jnp.float32).T
    grad_result = cotangent.T
    segments = segment_ids[0]
    padding = padding_mask[0]
    head_cols = w_qkv.shape[0] // (3 * width_share)
    heads_here = head_cols // HEAD
    qkv_block = w_qkv.reshape(width_share, 3, head_cols)
    qkv_flat = qkv_block.reshape(width_share, 3 * head_cols)
    out_block = w_out.reshape(-1, width_share)
    up_block = w_up.reshape(width_share, -1)
    down_block = w_down.reshape(-1, width_share)
    inverse_one, normed_one = norm_forward(inputs, gain_one)
    gathered_one, projected = project_in(normed_one, qkv_flat)
    length = projected.shape[0]
    projected = projected.reshape(length, 3, heads_here, HEAD)
    factor = LOG_TWO_E / math.sqrt(HEAD) * jnp.log1p(jnp.exp(scale_raw))
    query_raw = projected[:, 0]
    queries = (query_raw * factor).astype(jnp.bfloat16)
    key_heads = projected[:, 1].astype(jnp.bfloat16)
    values = projected[:, 2].astype(jnp.bfloat16)
    attended, log_totals = attention_forward(queries, key_heads, values, segments, padding)
    attended = attended.astype(jnp.bfloat16)
    gathered_att, branch_one = project_out(attended, out_block)
    middle = inputs + branch_one
    inverse_two, normed_two = norm_forward(middle, gain_two)
    gathered_two, hidden = project_in(normed_two, up_block)
    active = jax.nn.silu(hidden).astype(jnp.bfloat16)
    gathered_act, branch_two = project_out(active, down_block)
    result = middle + branch_two
    grad_active, grad_down = back_out(grad_result, gathered_act, down_block)
    sigmoid_hidden = jax.nn.sigmoid(hidden)
    grad_hidden = (grad_active * sigmoid_hidden * (1.0 + hidden * (1.0 - sigmoid_hidden))).astype(
        jnp.bfloat16
    )
    grad_normed_two, grad_up = back_in(grad_hidden, gathered_two, up_block)
    grad_mid_norm, gain_two_part = norm_backward(middle, inverse_two, gain_two, grad_normed_two)
    grad_middle = grad_result.astype(jnp.float32) + grad_mid_norm
    grad_attended, grad_wout = back_out(grad_middle.astype(jnp.bfloat16), gathered_att, out_block)
    grad_attended = grad_attended.reshape(length, heads_here, HEAD).astype(jnp.bfloat16)
    grad_queries, grad_keys, grad_values = attention_backward(
        queries, key_heads, values, segments, padding, log_totals, grad_attended
    )
    scale_part = (
        jnp.sum(grad_queries * query_raw, axis=(0, 1))
        * (LOG_TWO_E / math.sqrt(HEAD))
        * jax.nn.sigmoid(scale_raw)
    )
    grad_projected = jnp.stack([grad_queries * factor, grad_keys, grad_values], axis=1)
    grad_projected = grad_projected.reshape(length, -1).astype(jnp.bfloat16)
    grad_normed_one, grad_qkv = back_in(grad_projected, gathered_one, qkv_flat)
    grad_in_norm, gain_one_part = norm_backward(inputs, inverse_one, gain_one, grad_normed_one)
    grad_tokens = grad_middle + grad_in_norm
    grad_qkv, grad_wout, grad_up, grad_down = lax.psum(
        (grad_qkv, grad_wout, grad_up, grad_down), "dp"
    )
    blank = jnp.zeros((gain_attn.shape[0],), jnp.float32)
    full_one = lax.dynamic_update_slice_in_dim(blank, gain_one_part, feature_start, 0)
    full_two = lax.dynamic_update_slice_in_dim(blank, gain_two_part, feature_start, 0)
    sums_one, sums_two, sums_scale = lax.psum(
        (full_one, full_two, scale_part), ("dp", "row", "col")
    )
    return (
        result.T,
        grad_tokens.T,
        grad_qkv.reshape(-1),
        grad_wout.reshape(-1),
        grad_up.reshape(-1),
        grad_down.reshape(-1),
        sums_one,
        sums_two,
        sums_scale,
    )


def solution(mesh):
    return jax.shard_map(
        on_device,
        mesh=mesh,
        in_specs=(
            P("row", ("dp", "col")),
            P(("dp", "row"), None),
            P(("dp", "row"), None),
            P(("row", "col")),
            P(("row", "col")),
            P(("row", "col")),
            P(("row", "col")),
            P(),
            P(),
            P(),
            P("row", ("dp", "col")),
        ),
        out_specs=(
            P("row", ("dp", "col")),
            P("row", ("dp", "col")),
            P(("row", "col")),
            P(("row", "col")),
            P(("row", "col")),
            P(("row", "col")),
            P(),
            P(),
            P(),
        ),
        check_vma=False,
    )
```

profile of v0, /device:TPU:0, one launch (start us, length us, event | category | flops | bytes accessed | tf_op | source)
XLA Modules:
  0.0 1823.4 jit_solution(14980410813567560156)
XLA Ops:
  15.3 99.6 %all-gather.9.cloned.1.call-done = bf16[4096,640]{1,0:T(8,128)(2,1)} async-done(((bf16[1024,640]{1,0:T(8,128)(2,1)}), bf16[4096,640]{1,0:T(8,128)(2,1)}) %all-gather.9.cloned.1.call-update) | async-done | bytes 5242896 | tf_op jit(solution)/shard_map/all_gather | solution.py:24
  115.0 12.4 fusion.53
  128.1 23.1 %reduce-scatter.9.cloned.1.call-done = f32[2048,960]{0,1:T(8,128)} async-done(((f32[4096,960]{0,1:T(8,128)}), f32[2048,960]{0,1:T(8,128)}) %reduce-scatter.9.cloned.1.call-update) | async-done | bytes 7864336 | tf_op jit(solution)/shard_map/reduce_scatter | solution.py:32
  158.9 74.6 %while.27 = (s32[]{:T(128)}, bf16[4,512,4,80]{1,3,2,0:T(8,128)(2,1)}, f32[4,4,512]{2,1,0:T(4,128)}, s32[4]{0:T(128)S(1)}, s32[2048]{0:T(1024)S(1)}, /*index=5*/s...) while((s32[]{:T(128)}, ...), condition=%wide.region_6.7_spmd, body=%wide.region_3.6_spmd.sunk | while | flops 1386217984 | bytes 68712728 | solution.py:139
  237.9 12.1 all-gather.11.cloned.1.call-done
  250.0 9.0 fusion.54
  261.6 176.7 %reduce-scatter.11.cloned.1.call-done = f32[1024,640]{1,0:T(8,128)} async-done(((f32[4096,640]{1,0:T(8,128)}), f32[1024,640]{1,0:T(8,128)}) %reduce-scatter.11.cloned.1.call-update) | async-done | bytes 2621456 | tf_op jit(solution)/shard_map/reduce_scatter | solution.py:38
  449.2 90.2 %all-gather.17.cloned.1.call-done = bf16[4096,640]{1,0:T(8,128)(2,1)} async-done(((bf16[1024,640]{1,0:T(8,128)(2,1)}), bf16[4096,640]{1,0:T(8,128)(2,1)}) %all-gather.17.cloned.1.call-update) | async-done | bytes 5242896 | tf_op jit(solution)/shard_map/all_gather | solution.py:24
  539.5 7.0 fusion.57
  548.1 89.9 %all-gather.13.cloned.1.call-done = bf16[4096,640]{1,0:T(8,128)(2,1)} async-done(((bf16[1024,640]{1,0:T(8,128)(2,1)}), bf16[4096,640]{1,0:T(8,128)(2,1)}) %all-gather.13.cloned.1.call-update) | async-done | bytes 5242896 | tf_op jit(solution)/shard_map/all_gather | solution.py:24
  637.9 7.3 fusion.55
  645.3 6.5 reduce-scatter.17.cloned.1.call-done
  651.8 16.9 reduce-scatter.13.cloned.1.call-done
  674.9 11.7 all-gather.19.cloned.1.call-done
  686.6 9.0 fusion.58
  700.5 8.8 fusion.56
  709.4 172.7 %reduce-scatter.19.cloned.1.call-done = f32[1024,640]{1,0:T(8,128)} async-done(((f32[4096,640]{1,0:T(8,128)}), f32[1024,640]{1,0:T(8,128)}) %reduce-scatter.19.cloned.1.call-update) | async-done | bytes 2621456 | tf_op jit(solution)/shard_map/reduce_scatter | solution.py:38
  888.3 175.1 %reduce-scatter.15.cloned.1.call-done = f32[1024,640]{1,0:T(8,128)} async-done(((f32[4096,640]{1,0:T(8,128)}), f32[1024,640]{1,0:T(8,128)}) %reduce-scatter.15.cloned.1.call-update) | async-done | bytes 2621456 | tf_op jit(solution)/shard_map/reduce_scatter | solution.py:38
  1063.4 5.9 fusion.52
  1069.4 99.2 %all-gather.21.cloned.1.call-done = bf16[4096,640]{1,0:T(8,128)(2,1)} async-done(((bf16[1024,640]{1,0:T(8,128)(2,1)}), bf16[4096,640]{1,0:T(8,128)(2,1)}) %all-gather.21.cloned.1.call-update) | async-done | bytes 5242896 | tf_op jit(solution)/shard_map/all_gather | solution.py:24
  1168.6 7.0 fusion.59
  1175.8 11.7 reduce-scatter.21.cloned.1.call-done
  1190.4 275.3 %while.28 = (s32[]{:T(128)}, f32[2048,4,80]{0,2,1:T(8,128)}, f32[2048,4,80]{0,2,1:T(8,128)}, f32[4,512,4,80]{1,0,3,2:T(4,128)}, s32[4]{0:T(128)S(1)}, /*index=5*...) while((s32[]{:T(128)}, f32[2048,4,80]{0,2,1:T(8,128)}, ...), condition=%wide.region_19.20_spmd.clone, body=%wide.region_17.19_spmd.clone.sunk | while | flops 3414688256 | bytes 226712080 | solution.py:176
  1199.8 5.7 copy-done
  1205.5 7.0 fusion.131
  1212.5 12.4 multiply_reduce_fusion.6
  1224.9 12.0 multiply_convert_fusion.6
  1244.4 13.6 dynamic_update_slice.27
  1267.1 5.7 copy-done
  1272.9 7.9 fusion.131
  1280.7 12.4 multiply_reduce_fusion.6
  1293.1 12.0 multiply_convert_fusion.6
  1313.5 13.6 dynamic_update_slice.27
  1342.0 7.9 fusion.131
  1349.9 12.4 multiply_reduce_fusion.6
  1362.3 12.0 multiply_convert_fusion.6
  1382.6 13.6 dynamic_update_slice.27
  1411.1 7.9 fusion.131
  1419.0 12.4 multiply_reduce_fusion.6
  1431.4 12.0 multiply_convert_fusion.6
  1451.7 13.6 dynamic_update_slice.27
  1475.2 20.4 %all-gather.23.cloned.1.call-done = bf16[4096,960]{0,1:T(8,128)(2,1)} async-done(((bf16[2048,960]{0,1:T(8,128)(2,1)}), bf16[4096,960]{0,1:T(8,128)(2,1)}) %all-gather.23.cloned.1.call-update) | async-done | bytes 7864336 | tf_op jit(solution)/shard_map/all_gather | solution.py:28
  1495.6 11.7 fusion.60
  1509.0 6.3 fusion.63
  1530.3 9.9 fusion.61
  1554.7 132.0 %reduce-scatter.23.cloned.1.call-done = f32[1024,640]{1,0:T(8,128)} async-done(((f32[4096,640]{1,0:T(8,128)}), f32[1024,640]{1,0:T(8,128)}) %reduce-scatter.23.cloned.1.call-update) | async-done | bytes 2621456 | tf_op jit(solution)/shard_map/reduce_scatter | solution.py:38
  1700.9 41.6 %all-reduce = (f32[1280]{0:T(1024)}, f32[1280]{0:T(1024)}, f32[80]{0:T(128)}) all-reduce(f32[1280]{0:T(1024)S(1)} %dynamic_update_slice.17, f32[1280]{0:T(1024)S(1)} %dynamic_update_slice.18, f32[80]{0:T(128)S(1)} %divide_multiply_fusion), channel_id=1, replica_groups=mesh['dp'=4,'row'=2,'col'=4] {'dp','row','col'}, use_global_device_ids=true, to_apply=%region_28.29 | all-reduce | flops 2640 | bytes 21120 | tf_op jit(solution)/shard_map/psum | solution.py:257
  1742.6 67.9 %all-reduce.4.cloned.1.call-done = (f32[614400]{0:T(1024)}, f32[204800]{0:T(1024)}, f32[204800]{0:T(1024)}, f32[204800]{0:T(1024)}) async-done(((f32[614400]{0:T(1024)}, f32[204800]{0:T(1024)}, f32[204800]{0:T(1024)}, f32[204800]{0:T(1024)}), (f32[614400]{0:T(1024)}, f32[204800]{0:T(1024)}, f32[204800]{0:T(1024)}, f32[204800]{0:T(1024)})) %all-reduce.4.cloned.1.call-update) | async-done | bytes 4915216 | tf_op jit(solution)/shard_map/psum | solution.py:251
  (279 shorter events, 267.0 us)
Async XLA Ops:
  7.2 4.9 copy-start.28
  7.2 107.8 %all-gather.9.cloned.1.call-start = ((), (), s32[]{:S(2)}) async-start(), calls=%async_computation.8 | async-start | bytes 6553600 | tf_op jit(solution)/shard_map/all_gather | solution.py:24
  9.0 5.2 copy-start.4
  9.0 5.3 copy-start.15
  14.2 137.0 %reduce-scatter.9.cloned.1.call-start = ((), (), s32[]{:S(2)}) async-start(), calls=%async_computation.9 | async-start | bytes 23592960 | tf_op jit(solution)/shard_map/reduce_scatter | solution.py:32
  15.3 112.1 %copy-start.10 = (bf16[640,960]{1,0:T(8,128)(2,1)}, bf16[640,960]{1,0:T(8,128)(2,1)S(1)}, u32[]{:S(2)}) copy-start(bf16[640,960]{1,0:T(8,128)(2,1)S(1)} %reshape_reshape.3) | copy-start | bytes 3686404
  127.4 122.6 %all-gather.11.cloned.1.call-start = ((), (), s32[]{:S(2)}) async-start(), calls=%async_computation.10 | async-start | bytes 3932160 | tf_op jit(solution)/shard_map/all_gather | solution.py:28
  128.1 27.0 %copy-start.26 = (f32[80]{0:T(128)}, f32[80]{0:T(128)S(1)}, u32[]{:S(2)}) copy-start(f32[80]{0:T(128)S(1)} %log-plus-one_multiply_fusion) | copy-start | bytes 964
  167.7 4.0 copy-start.12
  186.4 4.0 copy-start.12
  205.1 4.0 copy-start.12
  223.7 4.0 copy-start.12
  237.3 201.0 %reduce-scatter.11.cloned.1.call-start = ((), (), s32[]{:S(2)}) async-start(), calls=%async_computation.11 | async-start | bytes 13107200 | tf_op jit(solution)/shard_map/reduce_scatter | solution.py:38
  259.0 280.4 %all-gather.17.cloned.1.call-start = ((), (), s32[]{:S(2)}) async-start(), calls=%async_computation.16 | async-start | bytes 6553600 | tf_op jit(solution)/shard_map/all_gather | solution.py:24
  261.5 376.4 %all-gather.13.cloned.1.call-start = ((), (), s32[]{:S(2)}) async-start(), calls=%async_computation.12 | async-start | bytes 6553600 | tf_op jit(solution)/shard_map/all_gather | solution.py:24
  447.8 204.0 %reduce-scatter.17.cloned.1.call-start = ((), (), s32[]{:S(2)}) async-start(), calls=%async_computation.17 | async-start | bytes 7864320 | tf_op jit(solution)/shard_map/reduce_scatter | solution.py:32
  449.2 97.3 %copy-start.6 = (bf16[320,640]{1,0:T(8,128)(2,1)}, bf16[320,640]{1,0:T(8,128)(2,1)S(1)}, u32[]{:S(2)}) copy-start(bf16[320,640]{1,0:T(8,128)(2,1)S(1)} %reshape.292) | copy-start | bytes 1228804
  546.5 122.2 %reduce-scatter.13.cloned.1.call-start = ((), (), s32[]{:S(2)}) async-start(), calls=%async_computation.13 | async-start | bytes 7864320 | tf_op jit(solution)/shard_map/reduce_scatter | solution.py:32
  645.3 41.3 %all-gather.19.cloned.1.call-start = ((), (), s32[]{:S(2)}) async-start(), calls=%async_computation.18 | async-start | bytes 3932160 | tf_op jit(solution)/shard_map/all_gather | solution.py:28
  673.9 26.7 %all-gather.15.cloned.1.call-start = ((), (), s32[]{:S(2)}) async-start(), calls=%async_computation.14 | async-start | bytes 3932160 | tf_op jit(solution)/shard_map/all_gather | solution.py:28
  674.5 207.6 %reduce-scatter.19.cloned.1.call-start = ((), (), s32[]{:S(2)}) async-start(), calls=%async_computation.19 | async-start | bytes 13107200 | tf_op jit(solution)/shard_map/reduce_scatter | solution.py:38
  695.6 4.9 copy-start.7
  695.6 367.8 %reduce-scatter.15.cloned.1.call-start = ((), (), s32[]{:S(2)}) async-start(), calls=%async_computation.15 | async-start | bytes 13107200 | tf_op jit(solution)/shard_map/reduce_scatter | solution.py:38
  709.4 459.3 %all-gather.21.cloned.1.call-start = ((), (), s32[]{:S(2)}) async-start(), calls=%async_computation.20 | async-start | bytes 6553600 | tf_op jit(solution)/shard_map/all_gather | solution.py:24
  1069.4 118.0 %reduce-scatter.21.cloned.1.call-start = ((), (), s32[]{:S(2)}) async-start(), calls=%async_computation.21 | async-start | bytes 7864320 | tf_op jit(solution)/shard_map/reduce_scatter | solution.py:32
  1175.7 319.9 %all-gather.23.cloned.1.call-start = ((), (), s32[]{:S(2)}) async-start(), calls=%async_computation.22 | async-start | bytes 11796480 | tf_op jit(solution)/shard_map/all_gather | solution.py:28
  1199.8 5.7 copy-start
  1243.7 14.3 copy-start.3
  1243.7 14.3 copy-start.33
  1267.1 5.7 copy-start
  1312.8 14.3 copy-start.3
  1312.8 14.3 copy-start.33
  1336.3 5.7 copy-start
  1381.9 14.3 copy-start.3
  1381.9 14.3 copy-start.33
  1405.4 5.7 copy-start
  1451.1 14.3 copy-start.3
  1451.1 14.3 copy-start.33
  1475.1 20.5 %copy-start.11 = (bf16[640,960]{1,0:T(8,128)(2,1)S(1)}, bf16[640,960]{1,0:T(8,128)(2,1)}, u32[]{:S(2)}) copy-start(bf16[640,960]{1,0:T(8,128)(2,1)} %copy-done.10) | copy-start | bytes 3686404
  1475.1 211.5 %reduce-scatter.23.cloned.1.call-start = ((), (), s32[]{:S(2)}) async-start(), calls=%async_computation.23 | async-start | bytes 13107200 | tf_op jit(solution)/shard_map/reduce_scatter | solution.py:38
  1507.3 303.1 %all-reduce.4.cloned.1.call-start = ((), (), s32[]{:S(2)}) async-start(), calls=%async_computation.24 | async-start | bytes 9830400 | tf_op jit(solution)/shard_map/psum | solution.py:251
  1518.1 6.6 copy-start.9
  1551.2 3.4 copy-start.31
  1551.2 135.4 %copy-start.5 = (bf16[640,1024]{0,1:T(8,128)(2,1)S(1)}, bf16[640,1024]{0,1:T(8,128)(2,1)}, u32[]{:S(2)}) copy-start(bf16[640,1024]{0,1:T(8,128)(2,1)} %copy-done.4) | copy-start | bytes 3932164
  1551.2 135.4 %copy-start.22 = (f32[1024]{0:T(1024)S(1)}, f32[1024]{0:T(1024)}, u32[]{:S(2)}) copy-start(f32[1024]{0:T(1024)} %copy-done.21) | copy-start | bytes 12292
  1551.2 135.4 %copy-start.24 = (f32[640]{0:T(1024)S(1)}, f32[640]{0:T(1024)}, u32[]{:S(2)}) copy-start(f32[640]{0:T(1024)} %copy-done.23) | copy-start | bytes 7684
  1810.5 3.4 copy-start.18
  1810.5 4.4 copy-start.17
  (24 other events, 38.0 us)
Sparse Core Ops, SparseCore 0:
  14.3 100.6 all-gather.8
  127.6 23.5 reduce-scatter.8
  237.5 12.4 all-gather.10
  259.1 179.1 reduce-scatter.10
  440.3 99.1 all-gather.16
  541.5 96.4 all-gather.12
  640.2 11.5 reduce-scatter.16
  654.2 14.4 reduce-scatter.12
  674.0 12.5 all-gather.18
  688.0 12.5 all-gather.14
  702.9 179.1 reduce-scatter.18
  884.3 179.0 reduce-scatter.14
  1069.5 99.0 all-gather.20
  1175.8 11.5 reduce-scatter.20
  1475.3 20.3 all-gather.22
  1507.5 179.1 reduce-scatter.22
  1691.3 119.0 all-reduce.3
where the time goes:
time: 1830 us; the launch traced here: 1820 us
  waiting for transfers between devices  1210 us (66%)
  matrix products  257 us (14%)
  other arithmetic  145 us (8%)
  local copies, waits for them, and re-layouts  136 us (7%)
  blocking collectives  51.7 us (3%)
    reduce_scatter x4, waiting for transfers between devices, sum_cols(): lax.psum_scatter(product(jnp.int32(0), number * lax.axis_size('col')), 'c...  656 us
    all_gather x4, waiting for transfers between devices, across_col(): return lax.all_gather(piece, 'col', axis=0, tiled=True)  379 us
    psum x1, waiting for transfers between devices, on_device(): lax.psum((grad_qkv, grad_wout, grad_up, grad_down), 'dp')  67.9 us
    reduce_scatter x4, waiting for transfers between devices, sum_rows(): lax.psum_scatter(product(jnp.int32(0), number * lax.axis_size('row')), 'r...  58.2 us
    dynamic_update_slice x8, local copies, waits for them, and re-layouts, attention_forward(): lax.map(one_block, jnp.arange(length // block_size, dtype=jnp.int32))  57 us
    dot_general x4, matrix products, one_block(): jnp.einsum('qhe,khe->hqk', grad_rows, values, preferred_element_type=jnp....  49.7 us
    all_gather x4, waiting for transfers between devices, across_row(): return lax.all_gather(piece, 'row', axis=0, tiled=True)  49.1 us
    convert_element_type x4, other arithmetic, one_block(): grad_scores = (probability * (grad_prob - inner)).astype(jnp.bfloat16)  47.9 us
  transfers between devices with their start and end apart: 17, of which 17 were waited for; matrix products, arithmetic and copies ran while one was open for 6% of the time, Pallas kernels for 0%

commit v1 on v0

v1 whole, which is shorter than its diff:
```python
import functools
import math

import jax
import jax.numpy as jnp
import numpy as np
from jax import lax
from jax.experimental import pallas as pl
from jax.experimental.pallas import tpu as pltpu
from jax.sharding import Mesh, PartitionSpec as P

D = 1280
HEAD = 80
EPSILON = 1e-06
LOG_TWO_E = 1.442695041
BLOCK = 256
LOW = jnp.bfloat16
FULL = jnp.float32
COLS = ("cs", "cp")


def mm(left, right, left_axis, right_axis):
    return lax.dot_general(
        left, right, (((left_axis,), (right_axis,)), ((), ())), preferred_element_type=FULL
    )


def shift(x, axis, k):
    n = lax.axis_size(axis)
    return lax.ppermute(x, axis, [(i, i ^ k) for i in range(n)])


def sibling(x):
    return shift(x, "row", 1)


def place(pieces, me, axis):
    n = len(pieces)
    if n == 1:
        return pieces[0]
    if n == 2:
        first = me == 0
        return jnp.concatenate(
            [jnp.where(first, pieces[0], pieces[1]), jnp.where(first, pieces[1], pieces[0])], axis
        )
    shape = list(pieces[0].shape)
    step = shape[axis]
    shape[axis] = step * n
    out = jnp.zeros(shape, pieces[0].dtype)
    for k, piece in enumerate(pieces):
        out = lax.dynamic_update_slice_in_dim(out, piece, (me ^ k) * step, axis)
    return out


def cut(x, index, count, axis):
    step = x.shape[axis] // count
    return lax.dynamic_slice_in_dim(x, index * step, step, axis)


def gather(x, axis):
    return [x] + [shift(x, axis, k) for k in range(1, lax.axis_size(axis))]


def swap(x, name, axis):
    me, n = lax.axis_index(name), lax.axis_size(name)
    parts = [cut(x, me ^ k, n, axis) for k in range(n)]
    return [parts[0]] + [shift(parts[k], name, k) for k in range(1, n)]


def reduce_pieces(pieces):
    total = pieces[0].astype(FULL)
    for piece in pieces[1:]:
        total = total + piece.astype(FULL)
    return total


def diag_mask(segq, segk):
    size = segk.shape[0], segq.shape[1]
    ki = lax.broadcasted_iota(jnp.int32, size, 0)
    qi = lax.broadcasted_iota(jnp.int32, size, 1)
    return ((segk == segq) & (ki <= qi)) | (ki == qi)


def forward_kernel(heads, lo_ref, hi_ref, q_ref, k_ref, v_ref, segq_ref, segk_ref, o_ref, log_ref, ks):
    i = pl.program_id(0)

    @pl.when(i == 0)
    def _():
        for h in range(heads):
            ks[h] = k_ref[h * HEAD:(h + 1) * HEAD, :].T

    segq = segq_ref[...]

    def visit(kb, carry, diagonal):
        at = pl.ds(pl.multiple_of(kb * BLOCK, BLOCK), BLOCK)
        segk = segk_ref[at, :]
        mask = diag_mask(segq, segk) if diagonal else segk == segq
        out = []
        for h in range(heads):
            rows = slice(h * HEAD, (h + 1) * HEAD)
            s = jnp.dot(ks[h, at, :], q_ref[rows, :], preferred_element_type=FULL)
            s = jnp.where(mask, s, -1e30)
            peak = jnp.max(s, axis=0, keepdims=True)
            if not diagonal:
                m, l, acc = carry[h]
                peak = jnp.maximum(m, peak)
            p = jnp.exp(s - peak)
            total = jnp.sum(p, axis=0, keepdims=True)
            new = jnp.dot(v_ref[rows, at], p.astype(LOW), preferred_element_type=FULL)
            if not diagonal:
                keep = jnp.exp(m - peak)
                total = l * keep + total
                new = acc * keep + new
            out.append((peak, total, new))
        return tuple(out)

    carry = visit(i, None, True)
    carry = lax.fori_loop(lo_ref[i], hi_ref[i], lambda kb, c: visit(kb, c, False), carry)
    for h in range(heads):
        m, l, acc = carry[h]
        o_ref[h * HEAD:(h + 1) * HEAD, :] = (acc / l).astype(LOW)
        log_ref[h] = m + jnp.log(l)


def attention_forward(q, k, v, segq, segk, lo, hi):
    cols, length = q.shape
    heads = cols // HEAD
    steps = length // BLOCK
    whole = pl.BlockSpec((cols, length), lambda i, *_: (0, 0))
    part = pl.BlockSpec((cols, BLOCK), lambda i, *_: (0, i))
    return pl.pallas_call(
        functools.partial(forward_kernel, heads),
        out_shape=(
            jax.ShapeDtypeStruct((cols, length), LOW),
            jax.ShapeDtypeStruct((heads, 1, length), FULL),
        ),
        grid_spec=pltpu.PrefetchScalarGridSpec(
            num_scalar_prefetch=2,
            grid=(steps,),
            in_specs=[
                part,
                whole,
                whole,
                pl.BlockSpec((1, BLOCK), lambda i, *_: (0, i)),
                pl.BlockSpec((length, 1), lambda i, *_: (0, 0)),
            ],
            out_specs=(part, pl.BlockSpec((heads, 1, BLOCK), lambda i, *_: (0, 0, i))),
            scratch_shapes=[pltpu.VMEM((heads, length, HEAD), LOW)],
        ),
        compiler_params=pltpu.CompilerParams(vmem_limit_bytes=48 * 2**20),
        cost_estimate=pl.CostEstimate(
            flops=8 * 2 * length * length * cols,
            bytes_accessed=4 * cols * length * 2,
            transcendentals=heads * length * length // 3,
        ),
    )(lo, hi, q, k, v, segq, segk)


def backward_kernel(
    heads, lo_ref, hi_ref, q_ref, k_ref, v_ref, o_ref, go_ref, log_ref, raw_ref, factor_ref,
    segq_ref, segk_ref, dq_ref, dk_ref, dv_ref, scale_ref, ks, vs, dks, dvs, dqs,
):
    i = pl.program_id(0)

    @pl.when(i == 0)
    def _():
        for h in range(heads):
            ks[h] = k_ref[h * HEAD:(h + 1) * HEAD, :].T
            vs[h] = v_ref[h * HEAD:(h + 1) * HEAD, :].T
        dks[...] = jnp.zeros_like(dks)
        dvs[...] = jnp.zeros_like(dvs)
        scale_ref[...] = jnp.zeros_like(scale_ref)

    segq = segq_ref[...]
    inner = [
        jnp.sum(
            o_ref[h * HEAD:(h + 1) * HEAD, :].astype(FULL)
            * go_ref[h * HEAD:(h + 1) * HEAD, :].astype(FULL),
            axis=0,
            keepdims=True,
        )
        for h in range(heads)
    ]

    def visit(kb, diagonal):
        at = pl.ds(pl.multiple_of(kb * BLOCK, BLOCK), BLOCK)
        segk = segk_ref[at, :]
        mask = diag_mask(segq, segk) if diagonal else segk == segq
        for h in range(heads):
            rows = slice(h * HEAD, (h + 1) * HEAD)
            q = q_ref[rows, :]
            go = go_ref[rows, :]
            s = jnp.dot(ks[h, at, :], q, preferred_element_type=FULL)
            p = jnp.where(mask, jnp.exp(s - log_ref[h]), 0.0)
            dp = jnp.dot(vs[h, at, :], go, preferred_element_type=FULL)
            ds = (p * (dp - inner[h])).astype(LOW)
            new = jnp.dot(k_ref[rows, at], ds, preferred_element_type=FULL)
            if diagonal:
                dqs[rows, :] = new
            else:
                dqs[rows, :] += new
            dks[rows, at] += mm(q, ds, 1, 1)
            dvs[rows, at] += mm(go, p.astype(LOW), 1, 1)

    visit(i, True)

    @pl.loop(lo_ref[i], hi_ref[i])
    def _(kb):
        visit(kb, False)

    factor = factor_ref[...]
    part = jnp.zeros((HEAD, 1), FULL)
    for h in range(heads):
        rows = slice(h * HEAD, (h + 1) * HEAD)
        dq = dqs[rows, :]
        part = part + jnp.sum(dq * raw_ref[rows, :], axis=1, keepdims=True)
        dq_ref[rows, :] = (dq * factor).astype(LOW)
    scale_ref[...] += part

    @pl.when(i == pl.num_programs(0) - 1)
    def _():
        dk_ref[...] = dks[...].astype(LOW)
        dv_ref[...] = dvs[...].astype(LOW)


def attention_backward(q, k, v, o, go, logs, raw, factor, segq, segk, lo, hi):
    cols, length = q.shape
    heads = cols // HEAD
    steps = length // BLOCK
    whole = pl.BlockSpec((cols, length), lambda i, *_: (0, 0))
    part = pl.BlockSpec((cols, BLOCK), lambda i, *_: (0, i))
    column = pl.BlockSpec((HEAD, 1), lambda i, *_: (0, 0))
    shape = jax.ShapeDtypeStruct((cols, length), LOW)
    return pl.pallas_call(
        functools.partial(backward_kernel, heads),
        out_shape=(shape, shape, shape, jax.ShapeDtypeStruct((HEAD, 1), FULL)),
        grid_spec=pltpu.PrefetchScalarGridSpec(
            num_scalar_prefetch=2,
            grid=(steps,),
            in_specs=[
                part,
                whole,
                whole,
                part,
                part,
                pl.BlockSpec((heads, 1, BLOCK), lambda i, *_: (0, 0, i)),
                part,
                column,
                pl.BlockSpec((1, BLOCK), lambda i, *_: (0, i)),
                pl.BlockSpec((length, 1), lambda i, *_: (0, 0)),
            ],
            out_specs=(part, whole, whole, column),
            scratch_shapes=[
                pltpu.VMEM((heads, length, HEAD), LOW),
                pltpu.VMEM((heads, length, HEAD), LOW),
                pltpu.VMEM((cols, length), FULL),
                pltpu.VMEM((cols, length), FULL),
                pltpu.VMEM((cols, BLOCK), FULL),
            ],
        ),
        compiler_params=pltpu.CompilerParams(vmem_limit_bytes=48 * 2**20),
        cost_estimate=pl.CostEstimate(
            flops=8 * 5 * length * length * cols,
            bytes_accessed=8 * cols * length * 2,
            transcendentals=heads * length * length // 3,
        ),
    )(lo, hi, q, k, v, o, go, logs, raw, factor, segq, segk)


def on_device(
    tokens,
    segment_ids,
    padding_mask,
    w_qkv,
    w_out,
    w_up,
    w_down,
    gain_attn,
    gain_mlp,
    scale_raw,
    cotangent,
):
    width, here = tokens.shape
    r, s = lax.axis_index("row"), lax.axis_index("cs")
    j, d = lax.axis_index("cp"), lax.axis_index("dp")
    n_pair, n_dp, n_col = lax.axis_size("cp"), lax.axis_size("dp"), lax.axis_size(COLS)
    c = s * n_pair + j
    head_cols = w_qkv.shape[0] // (3 * width)
    heads = head_cols // HEAD
    near = r == s

    segments = jnp.where(s == r, segment_ids[0], sibling(segment_ids)[0])
    padding = jnp.where(s == r, padding_mask[0], sibling(padding_mask)[0])
    length = segments.shape[0]
    firsts = segments[::BLOCK]
    starts = jnp.sum((segments[None, :] < firsts[:, None]).astype(jnp.int32), axis=1)
    filled = (jnp.sum(padding) + BLOCK - 1) // BLOCK
    blocks = jnp.arange(length // BLOCK, dtype=jnp.int32)
    lo = starts // BLOCK
    hi = jnp.minimum(blocks, filled)
    segq = segments[None, :]
    segk = jnp.where(padding == 1, segments, -1)[:, None]

    token_pieces = gather(tokens, "cp")
    token_others = [sibling(piece) for piece in token_pieces]
    grad_out = cotangent
    grad_out_full = jnp.concatenate([grad_out, sibling(grad_out)], 0)

    def halves(vector):
        whole = vector.reshape(2, width)
        own = lax.dynamic_index_in_dim(whole, r, 0, keepdims=False)
        other = lax.dynamic_index_in_dim(whole, 1 - r, 0, keepdims=False)
        return own[:, None], other[:, None]

    gain_one, gain_one_other = halves(gain_attn)
    gain_two, _ = halves(gain_mlp)

    block = w_qkv.reshape(width, 3 * head_cols)
    remote = place(gather(shift(cut(block, d, n_dp, 0), "cs", 1), "dp"), d, 0)
    qkv = jnp.concatenate(
        [jnp.where(near, block, remote), sibling(jnp.where(near, remote, block))], 0
    )

    stacked = jnp.stack([w_out.reshape(-1, width), w_up.reshape(width, -1).T, w_down.reshape(-1, width)])
    unit = stacked.shape[1]
    quarter = cut(stacked, d, n_dp, 1)[:, None, None]
    along_z = [quarter] + [
        lax.ppermute(quarter, COLS, [(i, i ^ k) for i in range(n_col)]) for k in range(1, n_col)
    ]
    c_first = c ^ (r * n_pair)
    along_z = place(along_z, c_first, 1)
    gathered = place(gather(along_z, "dp"), d, 2)
    gathered = gathered.reshape(3, n_col * unit, width)
    half_units = n_col * unit // 2
    crossed = sibling(gathered[:, half_units:])
    out_own, up_own, down_own = gathered
    out_half, up_half, down_half = jnp.concatenate([gathered[:, :half_units], crossed], 2)

    def project(own, other):
        own, other = own.astype(FULL), other.astype(FULL)
        squares = jnp.sum(own * own, axis=0) + jnp.sum(other * other, axis=0)
        inverse = lax.rsqrt(squares / D + EPSILON)[None, :]
        normed = jnp.concatenate(
            [
                (own * inverse * gain_one).astype(LOW),
                (other * inverse * gain_one_other).astype(LOW),
            ],
            0,
        )
        return inverse, normed, mm(qkv, normed, 0, 0)

    pieces = [project(own, other) for own, other in zip(token_pieces, token_others)]
    inverse_one = pieces[0][0]
    normed_one = place([piece[1] for piece in pieces], j, 1)
    projected = place([piece[2] for piece in pieces], j, 1)
    factor = (LOG_TWO_E / math.sqrt(HEAD) * jnp.log1p(jnp.exp(scale_raw)))[:, None]
    query_raw = projected[:head_cols]
    queries = (query_raw * jnp.tile(factor, (heads, 1))).astype(LOW)
    key_heads = projected[head_cols:2 * head_cols].astype(LOW)
    values = projected[2 * head_cols:].astype(LOW)

    attended, logs = attention_forward(queries, key_heads, values, segq, segk, lo, hi)
    mine = place(swap(attended, "cp", 1), j, 0)
    att_full = jnp.concatenate([mine, sibling(mine)], 0)

    inputs = tokens.astype(FULL)
    middle = inputs + mm(out_own, att_full, 0, 0)
    squares = jnp.sum(middle * middle, axis=0, keepdims=True)
    inverse_two = lax.rsqrt((squares + sibling(squares)) / D + EPSILON)
    normed_two = (middle * inverse_two * gain_two).astype(LOW)
    normed_full = jnp.concatenate([normed_two, sibling(normed_two)], 0)
    hidden = mm(up_half, normed_full, 1, 0)
    sigmoid = jax.nn.sigmoid(hidden)
    active = (hidden * sigmoid).astype(LOW)
    active_full = jnp.concatenate([active, sibling(active)], 0)
    result = middle + mm(down_own, active_full, 0, 0)

    grad_active = mm(down_half, grad_out_full, 1, 0)
    grad_hidden = (grad_active * sigmoid * (1.0 + hidden * (1.0 - sigmoid))).astype(LOW)
    grad_hidden_full = jnp.concatenate([grad_hidden, sibling(grad_hidden)], 0)
    grad_normed_two = mm(up_own, grad_hidden_full, 0, 0)
    scaled = grad_normed_two * gain_two
    inner = jnp.sum(scaled * middle, axis=0, keepdims=True)
    inner = inner + sibling(inner)
    grad_middle = (
        grad_out.astype(FULL)
        + inverse_two * scaled
        - middle * (inverse_two * inverse_two * inverse_two * inner / D)
    )
    gain_two_part = jnp.sum(grad_normed_two * middle * inverse_two, axis=1)
    grad_branch = grad_middle.astype(LOW)
    grad_branch_full = jnp.concatenate([grad_branch, sibling(grad_branch)], 0)
    grad_mine = mm(out_half, grad_branch_full, 1, 0).astype(LOW)
    grad_attended = place(swap(grad_mine, "cp", 0), j, 1)

    grads = jnp.stack(
        [
            mm(att_full, grad_branch, 1, 1).astype(LOW),
            mm(grad_hidden_full, normed_two, 1, 1).astype(LOW),
            mm(active_full, grad_out, 1, 1).astype(LOW),
        ]
    ).reshape(3, n_col, n_dp, unit // n_dp, width)
    summed = reduce_pieces(swap(grads, "dp", 2)).astype(LOW)
    parts = [
        lax.dynamic_slice_in_dim(summed, c_first ^ k, 1, 1) for k in range(n_col)
    ]
    parts = [parts[0]] + [
        lax.ppermute(parts[k], COLS, [(i, i ^ k) for i in range(n_col)]) for k in range(1, n_col)
    ]
    final = reduce_pieces(parts).astype(LOW)
    final = place(gather(final, "dp"), d, 2).astype(FULL).reshape(3, unit, width)

    dq, dk, dv, scale_part = attention_backward(
        queries, key_heads, values, attended, grad_attended, logs, query_raw, factor,
        segq, segk, lo, hi,
    )
    grad_projected = jnp.concatenate([dq, dk, dv], 0)

    grad_qkv = mm(normed_one, grad_projected, 1, 1).astype(LOW)
    grad_qkv = grad_qkv.reshape(2, n_dp, width // n_dp, 3 * head_cols)
    grad_qkv = reduce_pieces(swap(grad_qkv, "dp", 1))[:, 0].astype(LOW)
    crossed_grad = sibling(grad_qkv[1])
    stay = jnp.where(near, grad_qkv[0], crossed_grad).astype(FULL)
    leave = jnp.where(near, crossed_grad, grad_qkv[0])
    grad_qkv = (stay + shift(leave, "cs", 1).astype(FULL)).astype(LOW)
    grad_qkv = place(gather(grad_qkv, "dp"), d, 0).astype(FULL)

    grad_normed = mm(qkv, grad_projected, 1, 0)
    grad_normed = grad_normed[:width] + sibling(grad_normed[width:].astype(LOW)).astype(FULL)
    own_part = cut(grad_normed, j, n_pair, 1)
    for k in range(1, n_pair):
        own_part = own_part + shift(
            cut(grad_normed, j ^ k, n_pair, 1).astype(LOW), "cp", k
        ).astype(FULL)
    scaled = own_part * gain_one
    inner = jnp.sum(scaled * inputs, axis=0, keepdims=True)
    inner = inner + sibling(inner)
    grad_tokens = (
        grad_middle
        + inverse_one * scaled
        - inputs * (inverse_one * inverse_one * inverse_one * inner / D)
    )
    gain_one_part = jnp.sum(own_part * inputs * inverse_one, axis=1)

    scale_part = (
        scale_part[:, 0] * (LOG_TWO_E / math.sqrt(HEAD)) * jax.nn.sigmoid(scale_raw)
    )
    sums = jnp.stack(
        [gain_one_part, gain_two_part, jnp.pad(scale_part, (0, width - HEAD))]
    )
    for name in ("dp", "cs", "cp"):
        k = 1
        while k < lax.axis_size(name):
            sums = sums + shift(sums, name, k)
            k *= 2
    other = sibling(sums)
    first = r == 0
    gains = jnp.concatenate(
        [jnp.where(first, sums[:2], other[:2]), jnp.where(first, other[:2], sums[:2])], 1
    )
    scale_total = (sums[2] + other[2])[:HEAD]
    return (
        result,
        grad_tokens,
        grad_qkv.reshape(-1),
        final[0].reshape(-1),
        final[1].T.reshape(-1),
        final[2].reshape(-1),
        gains[0],
        gains[1],
        scale_total,
    )


def solution(mesh):
    n_dp, n_row, n_col = (mesh.shape[name] for name in ("dp", "row", "col"))
    split = Mesh(
        np.asarray(mesh.devices).reshape(n_dp, n_row, n_row, n_col // n_row),
        ("dp", "row", "cs", "cp"),
    )
    rows = P("row", ("dp", "cs", "cp"))
    ids = P(("dp", "row"), None)
    blocks = P(("row", "cs", "cp"))
    return jax.shard_map(
        on_device,
        mesh=split,
        in_specs=(rows, ids, ids, blocks, blocks, blocks, blocks, P(), P(), P(), rows),
        out_specs=(rows, rows, blocks, blocks, blocks, blocks, P(), P(), P()),
        check_vma=False,
    )
```

time: 1830 us -> 496 us (0.27)
  waiting for transfers between devices: 1210 us -> 196 us
  matrix products: 257 us -> 49.4 us
  other arithmetic: 145 us -> 46.3 us
  local copies, waits for them, and re-layouts: 136 us -> 68.2 us
  Pallas kernels: 0 us -> 63.1 us
  starting transfers between devices: 1.75 us -> 60.6 us
  blocking collectives: 51.7 us -> 0 us
    reduce_scatter x8 -> x0, waiting for transfers between devices: 715 us -> none  [the longest x4 656 us: sum_cols(): lax.psum_scatter(product(jnp.int32(0), number * lax.axis_size('col')), 'c...]
    all_gather x8 -> x0, waiting for transfers between devices: 428 us -> none  [the longest x4 379 us: across_col(): return lax.all_gather(piece, 'col', axis=0, tiled=True)]
    dot_general x40 -> x13, matrix products: 257 us -> 49.4 us  [mm(): lax.dot_general(left, right, (((left_axis,), (right_axis,)), ((), ())), p...]
    ppermute x0 -> x52, waiting for transfers between devices: none -> 196 us  [the longest x46 190 us: shift(): return lax.ppermute(x, axis, [(i, i ^ k) for i in range(n)])]
    psum x1 -> x0, waiting for transfers between devices: 67.9 us -> none  [on_device(): lax.psum((grad_qkv, grad_wout, grad_up, grad_down), 'dp')]
    pallas_call x0 -> x2, Pallas kernels: none -> 63.1 us  [the longest x1 33.8 us: attention_backward(): pl.pallas_call(functools.partial(backward_kernel, heads), out_shape=(shap...]
    ppermute x0 -> x52, starting transfers between devices: none -> 60.6 us  [the longest x46 47.6 us: shift(): return lax.ppermute(x, axis, [(i, i ^ k) for i in range(n)])]
    convert_element_type x10 -> x6, other arithmetic: 69.6 us -> 13.5 us  [the longest x1 3.47 us: project(): (own * inverse * gain_one).astype(LOW)]
  transfers between devices with their start and end apart: 17 -> 52, of which waited for: 17 -> 20; matrix products, arithmetic and copies ran while one was open for 6% -> 30% of each run, Pallas kernels for 0% -> 13%
where the time goes in v1:
time: 496 us; the launch traced here: 487 us
  waiting for transfers between devices  196 us (40%)
  local copies, waits for them, and re-layouts  68.2 us (14%)
  Pallas kernels  63.1 us (13%)
  starting transfers between devices  60.6 us (12%)
  matrix products  49.4 us (10%)
  other arithmetic  46.3 us (9%)
    ppermute x46, waiting for transfers between devices, shift(): return lax.ppermute(x, axis, [(i, i ^ k) for i in range(n)])  190 us
    dot_general x13, matrix products, mm(): lax.dot_general(left, right, (((left_axis,), (right_axis,)), ((), ())), p...  49.4 us
    ppermute x46, starting transfers between devices, shift(): return lax.ppermute(x, axis, [(i, i ^ k) for i in range(n)])  47.6 us
    pallas_call x1, Pallas kernels, attention_backward(): pl.pallas_call(functools.partial(backward_kernel, heads), out_shape=(shap...  33.8 us
    pallas_call x1, Pallas kernels, attention_forward(): pl.pallas_call(functools.partial(forward_kernel, heads), out_shape=(jax.S...  29.4 us
    dynamic_update_slice x17, local copies, waits for them, and re-layouts, place(): out = lax.dynamic_update_slice_in_dim(out, piece, (me ^ k) * step, axis)  11.7 us
  transfers between devices with their start and end apart: 52, of which 20 were waited for; matrix products, arithmetic and copies ran while one was open for 30% of the time, Pallas kernels for 13%

profile of v1, /device:TPU:0, one launch (start us, length us, event | category | flops | bytes accessed | tf_op | source)
XLA Modules:
  0.0 486.8 jit_solution(846837066670188075)
XLA Ops:
  1.2 3.0 collective-permute-start.14
  10.4 2.6 collective-permute-start.1
  13.0 3.5 reshape.186
  19.0 27.3 %collective-permute-done.8 = bf16[160,960]{1,0:T(8,128)(2,1)S(1)} collective-permute-done((bf16[160,960]{1,0:T(8,128)(2,1)S(1)}, bf16[160,960]{1,0:T(8,128)(2,1)S(1)}, u32[]{:S(2)}, u32[]{:S(2)}) %collective-permute-start.8) | collective-permute-done | bytes 307232 | tf_op jit(solution)/shard_map/ppermute | solution.py:30
  50.8 7.7 %collective-permute-done.9 = bf16[160,960]{1,0:T(8,128)(2,1)S(1)} collective-permute-done((bf16[160,960]{1,0:T(8,128)(2,1)S(1)}, bf16[160,960]{1,0:T(8,128)(2,1)S(1)}, u32[]{:S(2)}, u32[]{:S(2)}) %collective-permute-start.9) | collective-permute-done | bytes 307232 | tf_op jit(solution)/shard_map/ppermute | solution.py:30
  58.5 3.5 collective-permute-start
  63.5 3.1 broadcast_select_fusion.5
  70.4 2.5 collective-permute-start.2
  75.8 5.8 %collective-permute-done.2 = bf16[3,1,1,80,640]{4,3,2,1,0:T(8,128)(2,1)S(1)} collective-permute-done((bf16[3,1,1,80,640]{4,3,2,1,0:T(8,128)(2,1)S(1)}, bf16[3,1,1,80,640]{4,3,2,1,0:T(8,128)(2,1)S(1)}, u32[]{:S(2)}, u32[]{:S(2)}) %collective-permute-start.2) | collective-permute-done | bytes 307232 | tf_op jit(solution)/shard_map/ppermute | solution.py:328
  87.1 2.6 copy.46
  91.3 3.5 fusion.19
  94.9 2.8 fusion.56
  97.7 3.0 broadcast_select_fusion.3
  104.6 29.4 %shard_map.178 = (bf16[320,2048]{1,0:T(8,128)(2,1)S(1)}, f32[4,1,2048]{2,1,0:T(1,128)S(1)}) custom-call(s32[8]{0:T(128)S(1)} %get-tuple-element.82.lo_ref, s32[8]{0:T(128)S(1)} %get-tuple-element.83.hi_ref, bf16[320,2048]{1,0:T(8,128)(2,1)S(1)} %get-tuple-element.35.q_ref, bf16[320,2048]{1,0:T(8,128)(2,1)S(1)} %get-tuple-element.52.k_ref, ...), custom_call_target="tpu_custom_call" | custom-call | flops 21474836480 | bytes 5242880 | tf_op jit(solution)/shard_map/pallas_call | solution.py:131
  134.0 7.1 %collective-permute-start.16 = (bf16[320,1024]{1,0:T(8,128)(2,1)S(1)}, bf16[320,1024]{1,0:T(8,128)(2,1)}, u32[]{:S(2)}, u32[]{:S(2)}) collective-permute-start(bf16[320,1024]{1,0:T(8,128)(2,1)S(1)} %constant_dynamic-slice_fusion.11), channel_id=1, source_target_pairs={{0,1},{1,0},{2,3},{3,2},{4,5},{5,4},{6,7},{7,6},{8,9},{9,8},{10,11... | collective-permute-start | bytes 1966088 | tf_op jit(solution)/shard_map/ppermute | solution.py:30
  141.2 14.7 %collective-permute-done.16 = bf16[320,1024]{1,0:T(8,128)(2,1)} collective-permute-done((bf16[320,1024]{1,0:T(8,128)(2,1)S(1)}, bf16[320,1024]{1,0:T(8,128)(2,1)}, u32[]{:S(2)}, u32[]{:S(2)}) %collective-permute-start.16) | collective-permute-done | bytes 655392 | tf_op jit(solution)/shard_map/ppermute | solution.py:30
  161.0 35.2 %collective-permute-done.4 = bf16[3,4,1,80,640]{4,3,2,1,0:T(8,128)(2,1)} collective-permute-done((bf16[3,4,1,80,640]{4,3,2,1,0:T(8,128)(2,1)}, bf16[3,4,1,80,640]{4,3,2,1,0:T(8,128)(2,1)}, u32[]{:S(2)}, u32[]{:S(2)}) %collective-permute-start.4) | collective-permute-done | bytes 1228832 | tf_op jit(solution)/shard_map/ppermute | solution.py:30
  199.2 2.7 fusion.94
  204.0 3.5 multiply_reduce_fusion.2
  214.0 3.3 multiply_convert_fusion.1
  217.4 4.0 multiply_convert_fusion
  221.9 2.5 collective-permute-done.23
  224.5 2.9 multiply_reduce_fusion
  234.4 3.6 convolution_convert_fusion.2
  245.8 3.8 fusion.51
  251.9 20.5 %collective-permute-done.38 = bf16[3,4,1,80,640]{4,3,2,1,0:T(8,128)(2,1)} collective-permute-done((bf16[3,4,1,80,640]{4,3,2,1,0:T(8,128)(2,1)}, bf16[3,4,1,80,640]{4,3,2,1,0:T(8,128)(2,1)}, u32[]{:S(2)}, u32[]{:S(2)}) %collective-permute-start.38) | collective-permute-done | bytes 1228832 | tf_op jit(solution)/shard_map/ppermute | solution.py:30
  272.4 25.6 %collective-permute-done.40 = bf16[3,4,1,80,640]{4,3,2,1,0:T(8,128)(2,1)} collective-permute-done((bf16[3,4,1,80,640]{4,3,2,1,0:T(8,128)(2,1)}, bf16[3,4,1,80,640]{4,3,2,1,0:T(8,128)(2,1)}, u32[]{:S(2)}, u32[]{:S(2)}) %collective-permute-start.40) | collective-permute-done | bytes 1228832 | tf_op jit(solution)/shard_map/ppermute | solution.py:30
  299.4 3.0 add_convert_fusion
  302.9 3.8 collective-permute-start.43
  308.4 33.8 %shard_map.179 = (bf16[320,2048]{1,0:T(8,128)(2,1)S(1)}, bf16[320,2048]{1,0:T(8,128)(2,1)S(1)}, bf16[320,2048]{1,0:T(8,128)(2,1)S(1)}, f32[80,1]{1,0:T(8,128)S(1)}) custom-call(s32[8]{0:T(128)S(1)} %get-tuple-element.82.lo_ref, s32[8]{0:T(128)S(1)} %get-tuple-element.83.hi_ref, bf16[320,2048]{1,0:T(8,128)(2,1)} %copy-done, bf16[320,2048]{1,0:T(8,128)(2,1)} %copy-done.1, ...), custom_call_target="tpu_custom_call" | custom-call | flops 53687091200 | bytes 10485760 | tf_op jit(solution)/shard_map/pallas_call | solution.py:234
  344.0 5.7 %fusion.58 = f32[1280,2048]{1,0:T(8,128)S(1)} fusion(bf16[960,2048]{1,0:T(8,128)(2,1)S(1)} %constant_dynamic-update-slice_fusion.20, bf16[640,960]{1,0:T(8,128)(2,1)S(1)} %copy-done.28, bf16[640,960]{1,0:T(8,128)(2,1)S(1)} %copy-done.32), kind=kOutput, calls=%fused_computation.103 | convolution fusion | flops 5038080000 | bytes 16875520 | tf_op jit(solution)/shard_map/dot_general | solution.py:23
  358.2 7.0 %fusion.5 = bf16[1280,960]{0,1:T(8,128)(2,1)} fusion(bf16[960,2048]{1,0:T(8,128)(2,1)S(1)} %constant_dynamic-update-slice_fusion.20, bf16[1280,1024]{1,0:T(8,128)(2,1)S(1)} %get-tuple-element.42, bf16[1280,1024]{1,0:T(8,128)(2,1)S(1)} %get-tuple-element.41), kind=kOutput, calls=%fused_computation.21 | convolution fusion | flops 5044879360 | bytes 11632640 | tf_op jit(solution)/shard_map/dot_general | solution.py:23
  365.2 4.4 copy.50
  375.5 5.2 %fusion.50 = f32[640,1024]{1,0:T(8,128)} fusion(f32[640,1024]{1,0:T(8,128)S(1)} %copy-done.5, bf16[1280,640]{1,0:T(8,128)(2,1)} %bitcast.71, bf16[640,1024]{1,0:T(8,128)(2,1)} %copy-done.50, bf16[640,1024]{1,0:T(8,128)(2,1)S(1)} %copy-done.49), kind=kOutput, calls=%fused_computation.91 | convolution fusion | flops 1683619840 | bytes 9502720 | tf_op jit(solution)/shard_map/dot_general | solution.py:23
  380.8 3.0 collective-permute-start.46
  383.8 5.4 %collective-permute-done.30 = bf16[2,1,160,960]{3,2,1,0:T(8,128)(2,1)S(1)} collective-permute-done((bf16[2,1,160,960]{3,2,1,0:T(8,128)(2,1)S(1)}, bf16[2,1,160,960]{3,2,1,0:T(8,128)(2,1)S(1)}, u32[]{:S(2)}, u32[]{:S(2)}) %collective-permute-start.30) | collective-permute-done | bytes 614432 | tf_op jit(solution)/shard_map/ppermute | solution.py:30
  389.2 15.5 %collective-permute-done.32 = bf16[2,1,160,960]{3,2,1,0:T(8,128)(2,1)S(1)} collective-permute-done((bf16[2,1,160,960]{3,2,1,0:T(8,128)(2,1)S(1)}, bf16[2,1,160,960]{3,2,1,0:T(8,128)(2,1)S(1)}, u32[]{:S(2)}, u32[]{:S(2)}) %collective-permute-start.32) | collective-permute-done | bytes 614432 | tf_op jit(solution)/shard_map/ppermute | solution.py:30
  404.7 5.1 %collective-permute-done.31 = bf16[2,1,160,960]{3,2,1,0:T(8,128)(2,1)S(1)} collective-permute-done((bf16[2,1,160,960]{3,2,1,0:T(8,128)(2,1)S(1)}, bf16[2,1,160,960]{3,2,1,0:T(8,128)(2,1)S(1)}, u32[]{:S(2)}, u32[]{:S(2)}) %collective-permute-start.31) | collective-permute-done | bytes 614432 | tf_op jit(solution)/shard_map/ppermute | solution.py:30
  411.4 4.1 slice_add_fusion
  425.1 4.0 collective-permute-start.34
  429.3 12.8 %collective-permute-done.34 = bf16[160,960]{1,0:T(8,128)(2,1)S(1)} collective-permute-done((bf16[160,960]{1,0:T(8,128)(2,1)S(1)}, bf16[160,960]{1,0:T(8,128)(2,1)S(1)}, u32[]{:S(2)}, u32[]{:S(2)}) %collective-permute-start.34) | collective-permute-done | bytes 307232 | tf_op jit(solution)/shard_map/ppermute | solution.py:30
  447.7 3.3 fusion.23
  452.6 2.9 collective-permute-done.35
  456.3 4.9 %collective-permute-done.47 = f32[3,640]{1,0:T(4,128)S(1)} collective-permute-done((f32[3,640]{1,0:T(4,128)S(1)}, f32[3,640]{1,0:T(4,128)S(1)}, u32[]{:S(2)}, u32[]{:S(2)}) %collective-permute-start.47) | collective-permute-done | bytes 7712 | tf_op jit(solution)/shard_map/ppermute | solution.py:30
  462.4 2.5 collective-permute-done.48
  465.8 3.8 reshape.195
  469.6 7.4 %collective-permute-start.50 = (f32[3,640]{1,0:T(4,128)S(1)}, f32[3,640]{1,0:T(4,128)S(1)}, u32[]{:S(2)}, u32[]{:S(2)}) collective-permute-start(f32[3,640]{1,0:T(4,128)S(1)} %add.271), channel_id=1, source_target_pairs={{0,1},{1,0},{2,3},{3,2},{4,5},{5,4},{6,7},{7,6},{8,9},{9,8},{10,11... | collective-permute-start | bytes 23048 | tf_op jit(solution)/shard_map/ppermute | solution.py:30
  478.7 6.4 %fusion.21 = f32[640,1024]{1,0:T(8,128)} fusion(bf16[640,1024]{1,0:T(8,128)(2,1)} %param.11, f32[1024]{0:T(1024)S(1)} %bitcast.85, f32[640]{0:T(1024)S(1)} %copy-done.38, f32[1024]{0:T(1024)S(1)} %copy-done.34, bf16[640,1024]{1,0:T(8,128)(2,1)} %collective-permute-done.28, f32[640,2048]{1,0:T(8,128)} %copy-done.3, s32[]{:T(128)S(6)} %select_n.246, ...), kind=kLoop, calls=%fused_computation.44 | loop fusion | flops 9175040 | bytes 14439428 | tf_op jit(solution)/shard_map/sub | solution.py:439
  (291 shorter events, 110.0 us)
Async XLA Ops:
  0.6 47.2 %collective-permute-start.6 = (s32[1,2048]{1,0:T(1,128)}, s32[1,2048]{1,0:T(1,128)S(1)}, u32[]{:S(2)}, u32[]{:S(2)}) collective-permute-start(s32[1,2048]{1,0:T(1,128)} %param.12), channel_id=1, source_target_pairs={{0,4},{4,0},{1,5},{5,1},{2,6},{6,2},{3,7},{7,3},{8,12},{12,8},{9,1... | collective-permute-start | bytes 24584 | tf_op jit(solution)/shard_map/ppermute | solution.py:30
  1.2 48.2 %collective-permute-start.7 = (s32[1,2048]{1,0:T(1,128)}, s32[1,2048]{1,0:T(1,128)S(1)}, u32[]{:S(2)}, u32[]{:S(2)}) collective-permute-start(s32[1,2048]{1,0:T(1,128)} %param.13), channel_id=1, source_target_pairs={{0,4},{4,0},{1,5},{5,1},{2,6},{6,2},{3,7},{7,3},{8,12},{12,8},{9,1... | collective-permute-start | bytes 24584 | tf_op jit(solution)/shard_map/ppermute | solution.py:30
  1.2 62.2 %collective-permute-start.14 = (bf16[640,1024]{1,0:T(8,128)(2,1)}, bf16[640,1024]{1,0:T(8,128)(2,1)}, u32[]{:S(2)}, u32[]{:S(2)}) collective-permute-start(bf16[640,1024]{1,0:T(8,128)(2,1)} %param.11), channel_id=1, source_target_pairs={{0,1},{1,0},{2,3},{3,2},{4,5},{5,4},{6,7},{7,6},{8,9},{9,8},{10,11... | collective-permute-start | bytes 3932168 | tf_op jit(solution)/shard_map/ppermute | solution.py:30
  10.4 64.6 %collective-permute-start.1 = (bf16[3,1,1,80,640]{4,3,2,1,0:T(8,128)(2,1)S(1)}, bf16[3,1,1,80,640]{4,3,2,1,0:T(8,128)(2,1)S(1)}, u32[]{:S(2)}, u32[]{:S(2)}) collective-permute-start(bf16[3,1,1,80,640]{4,3,2,1,0:T(8,128)(2,1)S(1)} %get-tuple-element.38), channel_id=1, source_target_pairs={{0,2},{1,3},{2,0},{3,1},{4,6},{5,7},{6,4},{7,5},{8,10},{9,11},{10,... | collective-permute-start | bytes 921608 | tf_op jit(solution)/shard_map/ppermute | solution.py:328
  17.6 28.8 %collective-permute-start.8 = (bf16[160,960]{1,0:T(8,128)(2,1)S(1)}, bf16[160,960]{1,0:T(8,128)(2,1)S(1)}, u32[]{:S(2)}, u32[]{:S(2)}) collective-permute-start(bf16[160,960]{1,0:T(8,128)(2,1)S(1)} %constant_dynamic-slice_fusion.14), channel_id=1, source_target_pairs={{0,2},{2,0},{1,3},{3,1},{4,6},{6,4},{5,7},{7,5},{8,10},{10,8},{9,1... | collective-permute-start | bytes 921608 | tf_op jit(solution)/shard_map/ppermute | solution.py:30
  46.3 15.7 %collective-permute-start.10 = (bf16[160,960]{1,0:T(8,128)(2,1)S(1)}, bf16[160,960]{1,0:T(8,128)(2,1)S(1)}, u32[]{:S(2)}, u32[]{:S(2)}) collective-permute-start(bf16[160,960]{1,0:T(8,128)(2,1)S(1)} %collective-permute-done.8), channel_id=1, source_target_pairs={{0,16},{8,24},{16,0},{24,8},{1,17},{9,25},{17,1},{25,9},{2,18},{10... | collective-permute-start | bytes 921608 | tf_op jit(solution)/shard_map/ppermute | solution.py:30
  47.9 10.6 %collective-permute-start.9 = (bf16[160,960]{1,0:T(8,128)(2,1)S(1)}, bf16[160,960]{1,0:T(8,128)(2,1)S(1)}, u32[]{:S(2)}, u32[]{:S(2)}) collective-permute-start(bf16[160,960]{1,0:T(8,128)(2,1)S(1)} %collective-permute-done.8), channel_id=1, source_target_pairs={{0,8},{8,0},{16,24},{24,16},{1,9},{9,1},{17,25},{25,17},{2,10},{10... | collective-permute-start | bytes 921608 | tf_op jit(solution)/shard_map/ppermute | solution.py:30
  50.1 13.3 %collective-permute-start.11 = (bf16[160,960]{1,0:T(8,128)(2,1)S(1)}, bf16[160,960]{1,0:T(8,128)(2,1)S(1)}, u32[]{:S(2)}, u32[]{:S(2)}) collective-permute-start(bf16[160,960]{1,0:T(8,128)(2,1)S(1)} %collective-permute-done.8), channel_id=1, source_target_pairs={{0,24},{8,16},{16,8},{24,0},{1,25},{9,17},{17,9},{25,1},{2,26},{10... | collective-permute-start | bytes 921608 | tf_op jit(solution)/shard_map/ppermute | solution.py:30
  58.5 11.9 %collective-permute-start = (bf16[3,1,1,80,640]{4,3,2,1,0:T(8,128)(2,1)S(1)}, bf16[3,1,1,80,640]{4,3,2,1,0:T(8,128)(2,1)}, u32[]{:S(2)}, u32[]{:S(2)}) collective-permute-start(bf16[3,1,1,80,640]{4,3,2,1,0:T(8,128)(2,1)S(1)} %get-tuple-element.38), channel_id=1, source_target_pairs={{0,1},{1,0},{2,3},{3,2},{4,5},{5,4},{6,7},{7,6},{8,9},{9,8},{10,11... | collective-permute-start | bytes 921608 | tf_op jit(solution)/shard_map/ppermute | solution.py:328
  62.0 23.4 %collective-permute-start.13 = (bf16[640,1024]{1,0:T(8,128)(2,1)S(1)}, bf16[640,1024]{1,0:T(8,128)(2,1)}, u32[]{:S(2)}, u32[]{:S(2)}) collective-permute-start(bf16[640,1024]{1,0:T(8,128)(2,1)S(1)} %copy-done.7), channel_id=1, source_target_pairs={{0,4},{4,0},{1,5},{5,1},{2,6},{6,2},{3,7},{7,3},{8,12},{12,8},{9,1... | collective-permute-start | bytes 3932168 | tf_op jit(solution)/shard_map/ppermute | solution.py:30
  63.4 26.2 %collective-permute-start.15 = (bf16[640,1024]{1,0:T(8,128)(2,1)}, bf16[640,1024]{1,0:T(8,128)(2,1)}, u32[]{:S(2)}, u32[]{:S(2)}) collective-permute-start(bf16[640,1024]{1,0:T(8,128)(2,1)} %collective-permute-done.14), channel_id=1, source_target_pairs={{0,4},{4,0},{1,5},{5,1},{2,6},{6,2},{3,7},{7,3},{8,12},{12,8},{9,1... | collective-permute-start | bytes 3932168 | tf_op jit(solution)/shard_map/ppermute | solution.py:30
  69.1 18.0 %collective-permute-start.12 = (bf16[640,960]{0,1:T(8,128)(2,1)}, bf16[640,960]{0,1:T(8,128)(2,1)}, u32[]{:S(2)}, u32[]{:S(2)}) collective-permute-start(bf16[640,960]{0,1:T(8,128)(2,1)} %copy.45), channel_id=1, source_target_pairs={{0,4},{4,0},{1,5},{5,1},{2,6},{6,2},{3,7},{7,3},{8,12},{12,8},{9,1... | collective-permute-start | bytes 3686408 | tf_op jit(solution)/shard_map/ppermute | solution.py:30
  70.4 11.2 %collective-permute-start.2 = (bf16[3,1,1,80,640]{4,3,2,1,0:T(8,128)(2,1)S(1)}, bf16[3,1,1,80,640]{4,3,2,1,0:T(8,128)(2,1)S(1)}, u32[]{:S(2)}, u32[]{:S(2)}) collective-permute-start(bf16[3,1,1,80,640]{4,3,2,1,0:T(8,128)(2,1)S(1)} %get-tuple-element.38), channel_id=1, source_target_pairs={{0,3},{1,2},{2,1},{3,0},{4,7},{5,6},{6,5},{7,4},{8,11},{9,10},{10,... | collective-permute-start | bytes 921608 | tf_op jit(solution)/shard_map/ppermute | solution.py:328
  82.4 77.1 %collective-permute-start.3 = (bf16[3,4,1,80,640]{4,3,2,1,0:T(8,128)(2,1)}, bf16[3,4,1,80,640]{4,3,2,1,0:T(8,128)(2,1)}, u32[]{:S(2)}, u32[]{:S(2)}) collective-permute-start(bf16[3,4,1,80,640]{4,3,2,1,0:T(8,128)(2,1)} %constant_dynamic-update-slice_fusion.16), channel_id=1, source_target_pairs={{0,8},{8,0},{16,24},{24,16},{1,9},{9,1},{17,25},{25,17},{2,10},{10... | collective-permute-start | bytes 3686408 | tf_op jit(solution)/shard_map/ppermute | solution.py:30
  134.0 21.8 %collective-permute-start.16 = (bf16[320,1024]{1,0:T(8,128)(2,1)S(1)}, bf16[320,1024]{1,0:T(8,128)(2,1)}, u32[]{:S(2)}, u32[]{:S(2)}) collective-permute-start(bf16[320,1024]{1,0:T(8,128)(2,1)S(1)} %constant_dynamic-slice_fusion.11), channel_id=1, source_target_pairs={{0,1},{1,0},{2,3},{3,2},{4,5},{5,4},{6,7},{7,6},{8,9},{9,8},{10,11... | collective-permute-start | bytes 1966088 | tf_op jit(solution)/shard_map/ppermute | solution.py:30
  141.1 55.0 %collective-permute-start.4 = (bf16[3,4,1,80,640]{4,3,2,1,0:T(8,128)(2,1)}, bf16[3,4,1,80,640]{4,3,2,1,0:T(8,128)(2,1)}, u32[]{:S(2)}, u32[]{:S(2)}) collective-permute-start(bf16[3,4,1,80,640]{4,3,2,1,0:T(8,128)(2,1)} %constant_dynamic-update-slice_fusion.16), channel_id=1, source_target_pairs={{0,16},{8,24},{16,0},{24,8},{1,17},{9,25},{17,1},{25,9},{2,18},{10... | collective-permute-start | bytes 3686408 | tf_op jit(solution)/shard_map/ppermute | solution.py:30
  141.2 56.5 %collective-permute-start.5 = (bf16[3,4,1,80,640]{4,3,2,1,0:T(8,128)(2,1)}, bf16[3,4,1,80,640]{4,3,2,1,0:T(8,128)(2,1)}, u32[]{:S(2)}, u32[]{:S(2)}) collective-permute-start(bf16[3,4,1,80,640]{4,3,2,1,0:T(8,128)(2,1)} %constant_dynamic-update-slice_fusion.16), channel_id=1, source_target_pairs={{0,24},{8,16},{16,8},{24,0},{1,25},{9,17},{17,9},{25,1},{2,26},{10... | collective-permute-start | bytes 3686408 | tf_op jit(solution)/shard_map/ppermute | solution.py:30
  157.4 46.7 %collective-permute-start.17 = (bf16[640,1024]{1,0:T(8,128)(2,1)S(1)}, bf16[640,1024]{1,0:T(8,128)(2,1)S(1)}, u32[]{:S(2)}, u32[]{:S(2)}) collective-permute-start(bf16[640,1024]{1,0:T(8,128)(2,1)S(1)} %pad_maximum_fusion.15), channel_id=1, source_target_pairs={{0,4},{4,0},{1,5},{5,1},{2,6},{6,2},{3,7},{7,3},{8,12},{12,8},{9,1... | collective-permute-start | bytes 3932168 | tf_op jit(solution)/shard_map/ppermute | solution.py:30
  201.9 9.6 %collective-permute-start.18 = (bf16[3,640,640]{2,1,0:T(8,128)(2,1)}, bf16[3,640,640]{2,1,0:T(8,128)(2,1)}, u32[]{:S(2)}, u32[]{:S(2)}) collective-permute-start(bf16[3,640,640]{2,1,0:T(8,128)(2,1)} %get-tuple-element.49), channel_id=1, source_target_pairs={{0,4},{4,0},{1,5},{5,1},{2,6},{6,2},{3,7},{7,3},{8,12},{12,8},{9,1... | collective-permute-start | bytes 7372808 | tf_op jit(solution)/shard_map/ppermute | solution.py:30
  211.3 6.0 %collective-permute-start.22 = (bf16[640,1024]{1,0:T(8,128)(2,1)S(1)}, bf16[640,1024]{1,0:T(8,128)(2,1)S(1)}, u32[]{:S(2)}, u32[]{:S(2)}) collective-permute-start(bf16[640,1024]{1,0:T(8,128)(2,1)S(1)} %copy-done.13), channel_id=1, source_target_pairs={{0,4},{4,0},{1,5},{5,1},{2,6},{6,2},{3,7},{7,3},{8,12},{12,8},{9,1... | collective-permute-start | bytes 3932168 | tf_op jit(solution)/shard_map/ppermute | solution.py:30
  221.8 8.4 %collective-permute-start.21 = (bf16[640,1024]{1,0:T(8,128)(2,1)S(1)}, bf16[640,1024]{1,0:T(8,128)(2,1)S(1)}, u32[]{:S(2)}, u32[]{:S(2)}) collective-permute-start(bf16[640,1024]{1,0:T(8,128)(2,1)S(1)} %get-tuple-element.79), channel_id=1, source_target_pairs={{0,4},{4,0},{1,5},{5,1},{2,6},{6,2},{3,7},{7,3},{8,12},{12,8},{9,1... | collective-permute-start | bytes 3932168 | tf_op jit(solution)/shard_map/ppermute | solution.py:30
  227.4 5.1 %collective-permute-start.24 = (f32[1,1024]{1,0:T(1,128)S(1)}, f32[1,1024]{1,0:T(1,128)S(1)}, u32[]{:S(2)}, u32[]{:S(2)}) collective-permute-start(f32[1,1024]{1,0:T(1,128)S(1)} %bitcast.90), channel_id=1, source_target_pairs={{0,4},{4,0},{1,5},{5,1},{2,6},{6,2},{3,7},{7,3},{8,12},{12,8},{9,1... | collective-permute-start | bytes 12296 | tf_op jit(solution)/shard_map/ppermute | solution.py:30
  234.2 11.6 %collective-permute-start.25 = (bf16[640,1024]{1,0:T(8,128)(2,1)}, bf16[640,1024]{1,0:T(8,128)(2,1)}, u32[]{:S(2)}, u32[]{:S(2)}) collective-permute-start(bf16[640,1024]{1,0:T(8,128)(2,1)} %fusion.90), channel_id=1, source_target_pairs={{0,4},{4,0},{1,5},{5,1},{2,6},{6,2},{3,7},{7,3},{8,12},{12,8},{9,1... | collective-permute-start | bytes 3932168 | tf_op jit(solution)/shard_map/ppermute | solution.py:30
  242.3 30.2 %collective-permute-start.38 = (bf16[3,4,1,80,640]{4,3,2,1,0:T(8,128)(2,1)}, bf16[3,4,1,80,640]{4,3,2,1,0:T(8,128)(2,1)}, u32[]{:S(2)}, u32[]{:S(2)}) collective-permute-start(bf16[3,4,1,80,640]{4,3,2,1,0:T(8,128)(2,1)} %get-tuple-element.43), channel_id=1, source_target_pairs={{0,8},{8,0},{16,24},{24,16},{1,9},{9,1},{17,25},{25,17},{2,10},{10... | collective-permute-start | bytes 3686408 | tf_op jit(solution)/shard_map/ppermute | solution.py:30
  242.3 55.7 %collective-permute-start.40 = (bf16[3,4,1,80,640]{4,3,2,1,0:T(8,128)(2,1)}, bf16[3,4,1,80,640]{4,3,2,1,0:T(8,128)(2,1)}, u32[]{:S(2)}, u32[]{:S(2)}) collective-permute-start(bf16[3,4,1,80,640]{4,3,2,1,0:T(8,128)(2,1)} %get-tuple-element.44), channel_id=1, source_target_pairs={{0,24},{8,16},{16,8},{24,0},{1,25},{9,17},{17,9},{25,1},{2,26},{10... | collective-permute-start | bytes 3686408 | tf_op jit(solution)/shard_map/ppermute | solution.py:30
  244.0 55.4 %collective-permute-start.39 = (bf16[3,4,1,80,640]{4,3,2,1,0:T(8,128)(2,1)}, bf16[3,4,1,80,640]{4,3,2,1,0:T(8,128)(2,1)}, u32[]{:S(2)}, u32[]{:S(2)}) collective-permute-start(bf16[3,4,1,80,640]{4,3,2,1,0:T(8,128)(2,1)} %get-tuple-element.45), channel_id=1, source_target_pairs={{0,16},{8,24},{16,0},{24,8},{1,17},{9,25},{17,1},{25,9},{2,18},{10... | collective-permute-start | bytes 3686408 | tf_op jit(solution)/shard_map/ppermute | solution.py:30
  250.7 56.2 %collective-permute-start.26 = (bf16[320,1024]{1,0:T(8,128)(2,1)S(1)}, bf16[320,1024]{1,0:T(8,128)(2,1)S(1)}, u32[]{:S(2)}, u32[]{:S(2)}) collective-permute-start(bf16[320,1024]{1,0:T(8,128)(2,1)S(1)} %constant_dynamic-slice_fusion.9), channel_id=1, source_target_pairs={{0,1},{1,0},{2,3},{3,2},{4,5},{5,4},{6,7},{7,6},{8,9},{9,8},{10,11... | collective-permute-start | bytes 1966088 | tf_op jit(solution)/shard_map/ppermute | solution.py:30
  302.5 55.2 %collective-permute-start.41 = (bf16[3,1,1,80,640]{4,3,2,1,0:T(8,128)(2,1)S(1)}, bf16[3,1,1,80,640]{4,3,2,1,0:T(8,128)(2,1)S(1)}, u32[]{:S(2)}, u32[]{:S(2)}) collective-permute-start(bf16[3,1,1,80,640]{4,3,2,1,0:T(8,128)(2,1)S(1)} %get-tuple-element.65), channel_id=1, source_target_pairs={{0,1},{1,0},{2,3},{3,2},{4,5},{5,4},{6,7},{7,6},{8,9},{9,8},{10,11... | collective-permute-start | bytes 921608 | tf_op jit(solution)/shard_map/ppermute | solution.py:408
  302.9 54.8 %collective-permute-start.43 = (bf16[3,1,1,80,640]{4,3,2,1,0:T(8,128)(2,1)S(1)}, bf16[3,1,1,80,640]{4,3,2,1,0:T(8,128)(2,1)S(1)}, u32[]{:S(2)}, u32[]{:S(2)}) collective-permute-start(bf16[3,1,1,80,640]{4,3,2,1,0:T(8,128)(2,1)S(1)} %get-tuple-element.66), channel_id=1, source_target_pairs={{0,3},{1,2},{2,1},{3,0},{4,7},{5,6},{6,5},{7,4},{8,11},{9,10},{10,... | collective-permute-start | bytes 921608 | tf_op jit(solution)/shard_map/ppermute | solution.py:408
  306.7 51.0 %collective-permute-start.42 = (bf16[3,1,1,80,640]{4,3,2,1,0:T(8,128)(2,1)S(1)}, bf16[3,1,1,80,640]{4,3,2,1,0:T(8,128)(2,1)S(1)}, u32[]{:S(2)}, u32[]{:S(2)}) collective-permute-start(bf16[3,1,1,80,640]{4,3,2,1,0:T(8,128)(2,1)S(1)} %get-tuple-element.67), channel_id=1, source_target_pairs={{0,2},{1,3},{2,0},{3,1},{4,6},{5,7},{6,4},{7,5},{8,10},{9,11},{10,... | collective-permute-start | bytes 921608 | tf_op jit(solution)/shard_map/ppermute | solution.py:408
  351.6 59.8 %collective-permute-start.27 = (bf16[640,2048]{1,0:T(8,128)(2,1)}, bf16[640,2048]{1,0:T(8,128)(2,1)}, u32[]{:S(2)}, u32[]{:S(2)}) collective-permute-start(bf16[640,2048]{1,0:T(8,128)(2,1)} %slice.151), channel_id=1, source_target_pairs={{0,4},{4,0},{1,5},{5,1},{2,6},{6,2},{3,7},{7,3},{8,12},{12,8},{9,1... | collective-permute-start | bytes 7864328 | tf_op jit(solution)/shard_map/ppermute | solution.py:30
  358.1 22.7 %collective-permute-start.45 = (bf16[3,1,1,80,640]{4,3,2,1,0:T(8,128)(2,1)S(1)}, bf16[3,1,1,80,640]{4,3,2,1,0:T(8,128)(2,1)S(1)}, u32[]{:S(2)}, u32[]{:S(2)}) collective-permute-start(bf16[3,1,1,80,640]{4,3,2,1,0:T(8,128)(2,1)S(1)} %get-tuple-element.30), channel_id=1, source_target_pairs={{0,16},{8,24},{16,0},{24,8},{1,17},{9,25},{17,1},{25,9},{2,18},{10... | collective-permute-start | bytes 921608 | tf_op jit(solution)/shard_map/ppermute | solution.py:30
  358.2 16.8 %collective-permute-start.44 = (bf16[3,1,1,80,640]{4,3,2,1,0:T(8,128)(2,1)S(1)}, bf16[3,1,1,80,640]{4,3,2,1,0:T(8,128)(2,1)S(1)}, u32[]{:S(2)}, u32[]{:S(2)}) collective-permute-start(bf16[3,1,1,80,640]{4,3,2,1,0:T(8,128)(2,1)S(1)} %get-tuple-element.30), channel_id=1, source_target_pairs={{0,8},{8,0},{16,24},{24,16},{1,9},{9,1},{17,25},{25,17},{2,10},{10... | collective-permute-start | bytes 921608 | tf_op jit(solution)/shard_map/ppermute | solution.py:30
  371.5 17.7 %collective-permute-start.30 = (bf16[2,1,160,960]{3,2,1,0:T(8,128)(2,1)S(1)}, bf16[2,1,160,960]{3,2,1,0:T(8,128)(2,1)S(1)}, u32[]{:S(2)}, u32[]{:S(2)}) collective-permute-start(bf16[2,1,160,960]{3,2,1,0:T(8,128)(2,1)S(1)} %get-tuple-element.53), channel_id=1, source_target_pairs={{0,8},{8,0},{16,24},{24,16},{1,9},{9,1},{17,25},{25,17},{2,10},{10... | collective-permute-start | bytes 1843208 | tf_op jit(solution)/shard_map/ppermute | solution.py:30
  373.5 31.2 %collective-permute-start.32 = (bf16[2,1,160,960]{3,2,1,0:T(8,128)(2,1)S(1)}, bf16[2,1,160,960]{3,2,1,0:T(8,128)(2,1)S(1)}, u32[]{:S(2)}, u32[]{:S(2)}) collective-permute-start(bf16[2,1,160,960]{3,2,1,0:T(8,128)(2,1)S(1)} %get-tuple-element.54), channel_id=1, source_target_pairs={{0,24},{8,16},{16,8},{24,0},{1,25},{9,17},{17,9},{25,1},{2,26},{10... | collective-permute-start | bytes 1843208 | tf_op jit(solution)/shard_map/ppermute | solution.py:30
  375.0 34.8 %collective-permute-start.31 = (bf16[2,1,160,960]{3,2,1,0:T(8,128)(2,1)S(1)}, bf16[2,1,160,960]{3,2,1,0:T(8,128)(2,1)S(1)}, u32[]{:S(2)}, u32[]{:S(2)}) collective-permute-start(bf16[2,1,160,960]{3,2,1,0:T(8,128)(2,1)S(1)} %get-tuple-element.55), channel_id=1, source_target_pairs={{0,16},{8,24},{16,0},{24,8},{1,17},{9,25},{17,1},{25,9},{2,18},{10... | collective-permute-start | bytes 1843208 | tf_op jit(solution)/shard_map/ppermute | solution.py:30
  380.8 36.8 %collective-permute-start.46 = (bf16[3,1,1,80,640]{4,3,2,1,0:T(8,128)(2,1)S(1)}, bf16[3,1,1,80,640]{4,3,2,1,0:T(8,128)(2,1)S(1)}, u32[]{:S(2)}, u32[]{:S(2)}) collective-permute-start(bf16[3,1,1,80,640]{4,3,2,1,0:T(8,128)(2,1)S(1)} %get-tuple-element.30), channel_id=1, source_target_pairs={{0,24},{8,16},{16,8},{24,0},{1,25},{9,17},{17,9},{25,1},{2,26},{10... | collective-permute-start | bytes 921608 | tf_op jit(solution)/shard_map/ppermute | solution.py:30
  417.0 30.7 %collective-permute-start.28 = (bf16[640,1024]{1,0:T(8,128)(2,1)}, bf16[640,1024]{1,0:T(8,128)(2,1)}, u32[]{:S(2)}, u32[]{:S(2)}) collective-permute-start(bf16[640,1024]{1,0:T(8,128)(2,1)} %dynamic-slice_convert_fusion), channel_id=1, source_target_pairs={{0,1},{1,0},{2,3},{3,2},{4,5},{5,4},{6,7},{7,6},{8,9},{9,8},{10,11... | collective-permute-start | bytes 3932168 | tf_op jit(solution)/shard_map/ppermute | solution.py:30
  417.6 7.5 %collective-permute-start.33 = (bf16[160,960]{1,0:T(8,128)(2,1)S(1)}, bf16[160,960]{1,0:T(8,128)(2,1)S(1)}, u32[]{:S(2)}, u32[]{:S(2)}) collective-permute-start(bf16[160,960]{1,0:T(8,128)(2,1)S(1)} %slice_bitcast_fusion), channel_id=1, source_target_pairs={{0,4},{4,0},{1,5},{5,1},{2,6},{6,2},{3,7},{7,3},{8,12},{12,8},{9,1... | collective-permute-start | bytes 921608 | tf_op jit(solution)/shard_map/ppermute | solution.py:30
  425.1 17.0 %collective-permute-start.34 = (bf16[160,960]{1,0:T(8,128)(2,1)S(1)}, bf16[160,960]{1,0:T(8,128)(2,1)S(1)}, u32[]{:S(2)}, u32[]{:S(2)}) collective-permute-start(bf16[160,960]{1,0:T(8,128)(2,1)S(1)} %broadcast_select_fusion.10), channel_id=1, source_target_pairs={{0,2},{2,0},{1,3},{3,1},{4,6},{6,4},{5,7},{7,5},{8,10},{10,8},{9,1... | collective-permute-start | bytes 921608 | tf_op jit(solution)/shard_map/ppermute | solution.py:30
  444.2 17.5 %collective-permute-start.36 = (bf16[160,960]{1,0:T(8,128)(2,1)S(1)}, bf16[160,960]{1,0:T(8,128)(2,1)S(1)}, u32[]{:S(2)}, u32[]{:S(2)}) collective-permute-start(bf16[160,960]{1,0:T(8,128)(2,1)S(1)} %get-tuple-element.32), channel_id=1, source_target_pairs={{0,16},{8,24},{16,0},{24,8},{1,17},{9,25},{17,1},{25,9},{2,18},{10... | collective-permute-start | bytes 921608 | tf_op jit(solution)/shard_map/ppermute | solution.py:30
  444.9 10.6 %collective-permute-start.35 = (bf16[160,960]{1,0:T(8,128)(2,1)S(1)}, bf16[160,960]{1,0:T(8,128)(2,1)S(1)}, u32[]{:S(2)}, u32[]{:S(2)}) collective-permute-start(bf16[160,960]{1,0:T(8,128)(2,1)S(1)} %get-tuple-element.32), channel_id=1, source_target_pairs={{0,8},{8,0},{16,24},{24,16},{1,9},{9,1},{17,25},{25,17},{2,10},{10... | collective-permute-start | bytes 921608 | tf_op jit(solution)/shard_map/ppermute | solution.py:30
  446.3 18.7 %collective-permute-start.37 = (bf16[160,960]{1,0:T(8,128)(2,1)S(1)}, bf16[160,960]{1,0:T(8,128)(2,1)S(1)}, u32[]{:S(2)}, u32[]{:S(2)}) collective-permute-start(bf16[160,960]{1,0:T(8,128)(2,1)S(1)} %get-tuple-element.32), channel_id=1, source_target_pairs={{0,24},{8,16},{16,8},{24,0},{1,25},{9,17},{17,9},{25,1},{2,26},{10... | collective-permute-start | bytes 921608 | tf_op jit(solution)/shard_map/ppermute | solution.py:30
  451.1 10.1 %collective-permute-start.47 = (f32[3,640]{1,0:T(4,128)S(1)}, f32[3,640]{1,0:T(4,128)S(1)}, u32[]{:S(2)}, u32[]{:S(2)}) collective-permute-start(f32[3,640]{1,0:T(4,128)S(1)} %pad_maximum_fusion.24), channel_id=1, source_target_pairs={{0,8},{8,0},{16,24},{24,16},{1,9},{9,1},{17,25},{25,17},{2,10},{10... | collective-permute-start | bytes 23048 | tf_op jit(solution)/shard_map/ppermute | solution.py:30
  462.4 14.6 %collective-permute-start.29 = (f32[1,1024]{1,0:T(1,128)S(1)}, f32[1,1024]{1,0:T(1,128)S(1)}, u32[]{:S(2)}, u32[]{:S(2)}) collective-permute-start(f32[1,1024]{1,0:T(1,128)S(1)} %bitcast.86), channel_id=1, source_target_pairs={{0,4},{4,0},{1,5},{5,1},{2,6},{6,2},{3,7},{7,3},{8,12},{12,8},{9,1... | collective-permute-start | bytes 12296 | tf_op jit(solution)/shard_map/ppermute | solution.py:30
  465.0 4.7 collective-permute-start.49
  469.6 9.0 %collective-permute-start.50 = (f32[3,640]{1,0:T(4,128)S(1)}, f32[3,640]{1,0:T(4,128)S(1)}, u32[]{:S(2)}, u32[]{:S(2)}) collective-permute-start(f32[3,640]{1,0:T(4,128)S(1)} %add.271), channel_id=1, source_target_pairs={{0,1},{1,0},{2,3},{3,2},{4,5},{5,4},{6,7},{7,6},{8,9},{9,8},{10,11... | collective-permute-start | bytes 23048 | tf_op jit(solution)/shard_map/ppermute | solution.py:30
  478.7 6.5 %collective-permute-start.51 = (f32[3,640]{1,0:T(4,128)S(1)}, f32[3,640]{1,0:T(4,128)S(1)}, u32[]{:S(2)}, u32[]{:S(2)}) collective-permute-start(f32[3,640]{1,0:T(4,128)S(1)} %add.272), channel_id=1, source_target_pairs={{0,4},{4,0},{1,5},{5,1},{2,6},{6,2},{3,7},{7,3},{8,12},{12,8},{9,1... | collective-permute-start | bytes 23048 | tf_op jit(solution)/shard_map/ppermute | solution.py:30
  (59 other events, 712.8 us)
